TPU v7x, 512 devices: a whole 4x4x16 slice. The times are simulated.
512 devices in a mesh: dp: 128 (over z, y, x_lo), tensor: 4 (over x_hi, core).
Axes of the slice: x: 4 (x_hi: 2, x_lo: 2; x = x_hi * 2 + x_lo), y: 4, z: 16, core: 2. Of those that a mesh axis runs over, the one named last changes fastest.
Arguments:
- image_embed: bfloat16 [22528, 1152], P('dp', 'tensor'), may hold values from -8 to 8
- text_embed: bfloat16 [22528, 1152], P('dp', 'tensor'), may hold values from -8 to 8
- log_scale: float32 [1], replicated, may hold values from 3.7 to 4.6
- logit_bias: float32 [1], replicated, may hold values from -4 to -1
Outputs:
- grad_image: float32 [22528, 1152], P('dp', 'tensor')
- grad_text: float32 [22528, 1152], P('dp', 'tensor')
All inputs are finite; a program needn't handle non-finite values.
Results may differ from a plain program's by a relative error of at most 0.0058.
Values may be sent and summed in bfloat16 or wider, within the bound.
A program may use at most 64 MiB of HBM per device.

v0:
```python
import jax
import jax.numpy as jnp
from jax import lax
from jax.sharding import PartitionSpec as P


def shifted_2(value, axis, steps):
    count = lax.axis_size(axis)
    pairs = [(source, (source + steps) % count) for source in range(count)]
    return lax.ppermute(value, axis, pairs)


def unit_rows(embed):
    values = embed.astype(jnp.float32)
    row_norm = jnp.sqrt(jnp.sum(values * values, axis=1, keepdims=True) + 1e-06)
    return (row_norm, values / row_norm)


def project_back(unit_grad, unit_vec, row_norm):
    inner = jnp.sum(unit_vec * unit_grad, axis=1, keepdims=True)
    return (unit_grad - unit_vec * inner) / row_norm


def pair_terms(image_rows, text_rows, logit_scale, shift_value, positive):
    scores = lax.dot_general(
        image_rows, text_rows, (((1,), (1,)), ((), ())), preferred_element_type=jnp.float32
    )
    logits = logit_scale * scores + shift_value
    pair_grad = (jax.nn.sigmoid(logits) - positive).astype(jnp.bfloat16)
    to_image = jnp.dot(pair_grad, text_rows, preferred_element_type=jnp.float32)
    to_text = lax.dot_general(
        pair_grad, image_rows, (((0,), (0,)), ((), ())), preferred_element_type=jnp.float32
    )
    return (to_image, to_text)


def body(image_embed, text_embed, log_scale, logit_bias):
    image_full, text_full = (
        lax.all_gather(image_embed, "tensor", axis=1, tiled=True),
        lax.all_gather(text_embed, "tensor", axis=1, tiled=True),
    )
    image_norm, image_unit = unit_rows(image_full)
    text_norm, text_unit = unit_rows(text_full)
    image_bf = image_unit.astype(jnp.bfloat16)
    text_bf = text_unit.astype(jnp.bfloat16)
    logit_scale = jnp.exp(log_scale[0])
    shift_value = logit_bias[0]
    replicas = lax.axis_size("tensor")
    cycle_size = lax.axis_size("dp")
    span = min(4, cycle_size // replicas)
    visits = cycle_size // (replicas * span)
    replica = lax.axis_index("tensor")
    image_step = 1
    text_unit_hop = span * visits
    row_count = image_bf.shape[0]
    width = image_bf.shape[1]
    blocks = [image_bf]
    fetched = image_bf
    for slot in range(1, span):
        fetched = shifted_2(fetched, "dp", -image_step)
        blocks.append(fetched)
    image_stack = jnp.concatenate(blocks, axis=0)
    current = text_bf
    for bit_index in range(2):
        shifted = shifted_2(current, "dp", -(text_unit_hop << bit_index))
        current = jnp.where(replica >> bit_index & 1 == 1, shifted, current)
    row_ids = jnp.arange(row_count, dtype=jnp.int32)
    identity = (row_ids[:, None] == row_ids[None, :]).astype(jnp.float32)
    top_block = jnp.where(replica == 0, identity, jnp.zeros_like(identity))
    positive = jnp.concatenate(
        [top_block, jnp.zeros(((span - 1) * row_count, row_count), jnp.float32)], axis=0
    )
    to_image, carried = pair_terms(image_stack, current, logit_scale, shift_value, positive)

    def visit_step(step_index, visit_state):
        text_now, text_total, image_total = visit_state
        text_now = shifted_2(text_now, "dp", -span)
        text_total = shifted_2(text_total, "dp", -span)
        more_image, more_text = pair_terms(image_stack, text_now, logit_scale, shift_value, 0.0)
        return (text_now, text_total + more_text, image_total + more_image)

    current, carried, to_image = lax.fori_loop(1, visits, visit_step, (current, carried, to_image))
    carried = shifted_2(carried, "dp", span * (visits - 1))
    for bit_index in range(2):
        shifted = shifted_2(carried, "dp", text_unit_hop << bit_index)
        carried = jnp.where(replica >> bit_index & 1 == 1, shifted, carried)
    image_parts = to_image.reshape(span, row_count, width)
    image_total = image_parts[span - 1]
    for slot in range(span - 2, -1, -1):
        image_total = shifted_2(image_total, "dp", image_step) + image_parts[slot]
    image_grad = project_back(logit_scale * image_total, image_unit, image_norm)
    text_grad = project_back(logit_scale * carried, text_unit, text_norm)
    grad_image, grad_text = (
        lax.psum_scatter(image_grad, "tensor", scatter_dimension=1, tiled=True),
        lax.psum_scatter(text_grad, "tensor", scatter_dimension=1, tiled=True),
    )
    return (grad_image, grad_text)


def solution(mesh):
    placed = (P("dp", "tensor"), P("dp", "tensor"), P(), P())
    return jax.shard_map(
        body,
        mesh=mesh,
        in_specs=placed,
        out_specs=(P("dp", "tensor"), P("dp", "tensor")),
        check_vma=False,
    )
```

profile of v0, /device:TPU:1, one launch (start us, length us, event | category | flops | bytes accessed | tf_op | source)
XLA Modules:
  0.0 757.8 jit_solution(5288108000864881584)
XLA Ops:
  7.2 15.0 %all-gather.1 = bf16[4,288,176]{1,2,0:T(8,128)(2,1)S(1)} all-gather(bf16[1,288,176]{1,2,0:T(8,128)(2,1)} %bitcast.67), channel_id=1, replica_groups=mesh['dp'=128,'tensor'=4] {'tensor'}, dimensions={0}, use_global_device_ids=true | all-gather | bytes 506880 | tf_op jit(solution)/shard_map/all_gather | solution.py:39
  23.2 9.4 %collective-permute-start.4 = (bf16[176,1152]{1,0:T(8,128)(2,1)S(1)}, bf16[176,1152]{1,0:T(8,128)(2,1)S(1)}, u32[]{:S(2)}, u32[]{:S(2)}) collective-permute-start(bf16[176,1152]{1,0:T(8,128)(2,1)S(1)} %bitcast_convert_fusion), channel_id=1, source_target_pairs={{0,508},{4,0},{8,4},{12,8},{16,12},{20,16},{24,20},{28,24},{32,28}... | collective-permute-start | bytes 1216520 | tf_op jit(solution)/shard_map/ppermute | solution.py:10
  32.7 8.9 %all-gather = bf16[4,288,176]{1,2,0:T(8,128)(2,1)S(1)} all-gather(bf16[1,288,176]{1,2,0:T(8,128)(2,1)S(1)} %bitcast.68), channel_id=1, replica_groups=mesh['dp'=128,'tensor'=4] {'tensor'}, dimensions={0}, use_global_device_ids=true | all-gather | bytes 506880 | tf_op jit(solution)/shard_map/all_gather | solution.py:40
  42.6 11.9 %collective-permute-start.2 = (bf16[176,1152]{1,0:T(8,128)(2,1)S(1)}, bf16[176,1152]{1,0:T(8,128)(2,1)S(1)}, u32[]{:S(2)}, u32[]{:S(2)}) collective-permute-start(bf16[176,1152]{1,0:T(8,128)(2,1)S(1)} %bitcast_convert_fusion.1), channel_id=1, source_target_pairs={{0,384},{4,388},{8,392},{12,396},{16,400},{20,404},{24,408},{28,41... | collective-permute-start | bytes 1216520 | tf_op jit(solution)/shard_map/ppermute | solution.py:10
  54.5 2.6 collective-permute-start.5
  57.1 31.8 %collective-permute-done.2 = bf16[176,1152]{1,0:T(8,128)(2,1)S(1)} collective-permute-done((bf16[176,1152]{1,0:T(8,128)(2,1)S(1)}, bf16[176,1152]{1,0:T(8,128)(2,1)S(1)}, u32[]{:S(2)}, u32[]{:S(2)}) %collective-permute-start.2) | collective-permute-done | bytes 405536 | tf_op jit(solution)/shard_map/ppermute | solution.py:10
  89.1 9.2 %collective-permute-start.3 = (bf16[176,1152]{1,0:T(8,128)(2,1)S(1)}, bf16[176,1152]{1,0:T(8,128)(2,1)S(1)}, u32[]{:S(2)}, u32[]{:S(2)}) collective-permute-start(bf16[176,1152]{1,0:T(8,128)(2,1)S(1)} %broadcast_select_fusion.1), channel_id=1, source_target_pairs={{0,256},{4,260},{8,264},{12,268},{16,272},{20,276},{24,280},{28,28... | collective-permute-start | bytes 1216520 | tf_op jit(solution)/shard_map/ppermute | solution.py:10
  99.6 25.5 %collective-permute-done.5 = bf16[176,1152]{1,0:T(8,128)(2,1)S(1)} collective-permute-done((bf16[176,1152]{1,0:T(8,128)(2,1)S(1)}, bf16[176,1152]{1,0:T(8,128)(2,1)S(1)}, u32[]{:S(2)}, u32[]{:S(2)}) %collective-permute-start.5) | collective-permute-done | bytes 405536 | tf_op jit(solution)/shard_map/ppermute | solution.py:10
  125.1 8.8 %collective-permute-start.6 = (bf16[176,1152]{1,0:T(8,128)(2,1)S(1)}, bf16[176,1152]{1,0:T(8,128)(2,1)S(1)}, u32[]{:S(2)}, u32[]{:S(2)}) collective-permute-start(bf16[176,1152]{1,0:T(8,128)(2,1)S(1)} %collective-permute-done.5), channel_id=1, source_target_pairs={{0,508},{4,0},{8,4},{12,8},{16,12},{20,16},{24,20},{28,24},{32,28}... | collective-permute-start | bytes 1216520 | tf_op jit(solution)/shard_map/ppermute | solution.py:10
  134.1 9.7 %collective-permute-done.6 = bf16[176,1152]{1,0:T(8,128)(2,1)S(1)} collective-permute-done((bf16[176,1152]{1,0:T(8,128)(2,1)S(1)}, bf16[176,1152]{1,0:T(8,128)(2,1)S(1)}, u32[]{:S(2)}, u32[]{:S(2)}) %collective-permute-start.6) | collective-permute-done | bytes 405536 | tf_op jit(solution)/shard_map/ppermute | solution.py:10
  147.2 229.9 %while.14 = (s32[]{:T(128)}, bf16[176,1152]{1,0:T(8,128)(2,1)}, f32[176,1152]{1,0:T(8,128)}, f32[704,1152]{1,0:T(8,128)S(1)}, f32[]{:T(128)}, /*index=5*/bf16[704,1152]{1,0:T(8,128)(2,1)}, f32[]{:T(128)}, s32[]{:T(128)}) while((s32[]{:T(128)}, bf16[176,1152]{1,0:T(8,128)(2,1)}, f32[176,1152]{1,0:T(8,128)}, f32[704,1152]{1,0:T(8,128)S(1)}, ...), condition=%wide.region_3.4_spmd, body=%wide.region_2.3_spmd.sunk | while | flops 858181632 | bytes 25073864 | solution.py:82
  149.1 5.3 collective-permute-start.1
  154.4 6.4 collective-permute-done
  162.6 2.8 fusion.46
  165.5 2.1 convolution_add_fusion.5
  167.6 10.6 %collective-permute-done.1 = f32[176,1152]{1,0:T(8,128)} collective-permute-done((f32[176,1152]{1,0:T(8,128)}, f32[176,1152]{1,0:T(8,128)}, u32[]{:S(2)}, u32[]{:S(2)}) %collective-permute-start.1) | collective-permute-done | bytes 811040 | tf_op jit(solution)/shard_map/while/body/eval_jaxpr/ppermute | solution.py:10
  178.2 2.6 convolution_add_fusion.4
  180.8 4.3 collective-permute-start
  185.1 3.4 collective-permute-start.1
  188.6 4.9 collective-permute-done
  195.3 2.8 fusion.46
  198.1 2.1 convolution_add_fusion.5
  200.3 10.6 %collective-permute-done.1 = f32[176,1152]{1,0:T(8,128)} collective-permute-done((f32[176,1152]{1,0:T(8,128)}, f32[176,1152]{1,0:T(8,128)}, u32[]{:S(2)}, u32[]{:S(2)}) %collective-permute-start.1) | collective-permute-done | bytes 811040 | tf_op jit(solution)/shard_map/while/body/eval_jaxpr/ppermute | solution.py:10
  210.8 2.6 convolution_add_fusion.4
  213.4 6.8 collective-permute-start
  222.1 4.5 collective-permute-done
  228.4 2.8 fusion.46
  231.3 2.1 convolution_add_fusion.5
  233.4 10.6 %collective-permute-done.1 = f32[176,1152]{1,0:T(8,128)} collective-permute-done((f32[176,1152]{1,0:T(8,128)}, f32[176,1152]{1,0:T(8,128)}, u32[]{:S(2)}, u32[]{:S(2)}) %collective-permute-start.1) | collective-permute-done | bytes 811040 | tf_op jit(solution)/shard_map/while/body/eval_jaxpr/ppermute | solution.py:10
  244.0 2.6 convolution_add_fusion.4
  246.6 7.7 %collective-permute-start = (bf16[176,1152]{1,0:T(8,128)(2,1)}, bf16[176,1152]{1,0:T(8,128)(2,1)}, u32[]{:S(2)}, u32[]{:S(2)}) collective-permute-start(bf16[176,1152]{1,0:T(8,128)(2,1)} %get-tuple-element.108), channel_id=1, source_target_pairs={{0,496},{4,500},{8,504},{12,508},{16,0},{20,4},{24,8},{28,12},{32,... | collective-permute-start | bytes 1216520 | tf_op jit(solution)/shard_map/while/body/eval_jaxpr/ppermute | solution.py:10
  256.2 3.6 collective-permute-done
  261.6 2.8 fusion.46
  264.5 2.1 convolution_add_fusion.5
  266.6 10.6 %collective-permute-done.1 = f32[176,1152]{1,0:T(8,128)} collective-permute-done((f32[176,1152]{1,0:T(8,128)}, f32[176,1152]{1,0:T(8,128)}, u32[]{:S(2)}, u32[]{:S(2)}) %collective-permute-start.1) | collective-permute-done | bytes 811040 | tf_op jit(solution)/shard_map/while/body/eval_jaxpr/ppermute | solution.py:10
  277.2 2.6 convolution_add_fusion.4
  279.8 7.7 %collective-permute-start = (bf16[176,1152]{1,0:T(8,128)(2,1)}, bf16[176,1152]{1,0:T(8,128)(2,1)}, u32[]{:S(2)}, u32[]{:S(2)}) collective-permute-start(bf16[176,1152]{1,0:T(8,128)(2,1)} %get-tuple-element.108), channel_id=1, source_target_pairs={{0,496},{4,500},{8,504},{12,508},{16,0},{20,4},{24,8},{28,12},{32,... | collective-permute-start | bytes 1216520 | tf_op jit(solution)/shard_map/while/body/eval_jaxpr/ppermute | solution.py:10
  289.4 3.2 collective-permute-done
  294.5 2.8 fusion.46
  297.3 2.1 convolution_add_fusion.5
  299.5 10.0 %collective-permute-done.1 = f32[176,1152]{1,0:T(8,128)} collective-permute-done((f32[176,1152]{1,0:T(8,128)}, f32[176,1152]{1,0:T(8,128)}, u32[]{:S(2)}, u32[]{:S(2)}) %collective-permute-start.1) | collective-permute-done | bytes 811040 | tf_op jit(solution)/shard_map/while/body/eval_jaxpr/ppermute | solution.py:10
  309.5 2.6 convolution_add_fusion.4
  312.1 7.7 %collective-permute-start = (bf16[176,1152]{1,0:T(8,128)(2,1)}, bf16[176,1152]{1,0:T(8,128)(2,1)}, u32[]{:S(2)}, u32[]{:S(2)}) collective-permute-start(bf16[176,1152]{1,0:T(8,128)(2,1)} %get-tuple-element.108), channel_id=1, source_target_pairs={{0,496},{4,500},{8,504},{12,508},{16,0},{20,4},{24,8},{28,12},{32,... | collective-permute-start | bytes 1216520 | tf_op jit(solution)/shard_map/while/body/eval_jaxpr/ppermute | solution.py:10
  321.7 3.2 collective-permute-done
  326.7 2.8 fusion.46
  329.6 2.1 convolution_add_fusion.5
  331.8 10.5 %collective-permute-done.1 = f32[176,1152]{1,0:T(8,128)} collective-permute-done((f32[176,1152]{1,0:T(8,128)}, f32[176,1152]{1,0:T(8,128)}, u32[]{:S(2)}, u32[]{:S(2)}) %collective-permute-start.1) | collective-permute-done | bytes 811040 | tf_op jit(solution)/shard_map/while/body/eval_jaxpr/ppermute | solution.py:10
  342.2 2.6 convolution_add_fusion.4
  344.8 6.3 collective-permute-start
  353.1 3.2 collective-permute-done
  358.1 2.8 fusion.46
  361.0 2.1 convolution_add_fusion.5
  363.1 11.4 %collective-permute-done.1 = f32[176,1152]{1,0:T(8,128)} collective-permute-done((f32[176,1152]{1,0:T(8,128)}, f32[176,1152]{1,0:T(8,128)}, u32[]{:S(2)}, u32[]{:S(2)}) %collective-permute-start.1) | collective-permute-done | bytes 811040 | tf_op jit(solution)/shard_map/while/body/eval_jaxpr/ppermute | solution.py:10
  374.5 2.6 convolution_add_fusion.4
  377.1 2.1 collective-permute-start.7
  381.1 35.7 %collective-permute-done.7 = f32[176,1152]{1,0:T(8,128)S(1)} collective-permute-done((f32[176,1152]{1,0:T(8,128)S(1)}, f32[176,1152]{1,0:T(8,128)S(1)}, u32[]{:S(2)}, u32[]{:S(2)}) %collective-permute-start.7) | collective-permute-done | bytes 811040 | tf_op jit(solution)/shard_map/ppermute | solution.py:10
  418.8 30.7 %collective-permute-done.10 = f32[176,1152]{1,0:T(8,128)S(1)} collective-permute-done((f32[176,1152]{1,0:T(8,128)S(1)}, f32[176,1152]{1,0:T(8,128)S(1)}, u32[]{:S(2)}, u32[]{:S(2)}) %collective-permute-start.10) | collective-permute-done | bytes 811040 | tf_op jit(solution)/shard_map/ppermute | solution.py:10
  449.5 2.8 collective-permute-start.11
  452.4 46.7 %collective-permute-done.8 = f32[176,1152]{1,0:T(8,128)S(1)} collective-permute-done((f32[176,1152]{1,0:T(8,128)S(1)}, f32[176,1152]{1,0:T(8,128)S(1)}, u32[]{:S(2)}, u32[]{:S(2)}) %collective-permute-start.8) | collective-permute-done | bytes 811040 | tf_op jit(solution)/shard_map/ppermute | solution.py:10
  502.3 10.8 %collective-permute-start.12 = (f32[176,1152]{1,0:T(8,128)}, f32[176,1152]{1,0:T(8,128)}, u32[]{:S(2)}, u32[]{:S(2)}) collective-permute-start(f32[176,1152]{1,0:T(8,128)} %broadcast_select_fusion), channel_id=1, source_target_pairs={{0,256},{4,260},{8,264},{12,268},{16,272},{20,276},{24,280},{28,28... | collective-permute-start | bytes 2433032 | tf_op jit(solution)/shard_map/ppermute | solution.py:10
  513.1 62.9 %collective-permute-done.9 = f32[176,1152]{1,0:T(8,128)S(1)} collective-permute-done((f32[176,1152]{1,0:T(8,128)S(1)}, f32[176,1152]{1,0:T(8,128)S(1)}, u32[]{:S(2)}, u32[]{:S(2)}) %collective-permute-start.9) | collective-permute-done | bytes 811040 | tf_op jit(solution)/shard_map/ppermute | solution.py:10
  577.5 2.6 copy.10
  584.4 113.7 %reduce-scatter.7.cloned.1.call-done = f32[288,176]{1,0:T(8,128)} async-done(((f32[1152,176]{1,0:T(8,128)}), f32[288,176]{1,0:T(8,128)}) %reduce-scatter.7.cloned.1.call-update) | async-done | bytes 202768
  699.9 49.2 %reduce-scatter.9.cloned.1.call-done = f32[288,176]{1,0:T(8,128)} async-done(((f32[1152,176]{1,0:T(8,128)}), f32[288,176]{1,0:T(8,128)}) %reduce-scatter.9.cloned.1.call-update) | async-done | bytes 202768
  (82 shorter events, 46.5 us)
Async XLA Ops:
  7.2 691.0 %reduce-scatter.7.cloned.1.call-start = ((), (), s32[]{:S(2)}) async-start(), calls=%async_computation.2 | async-start | bytes 1474560
  22.4 10.3 %copy-start.8 = (bf16[176,288]{1,0:T(8,128)(2,1)S(1)}, bf16[176,288]{1,0:T(8,128)(2,1)}, u32[]{:S(2)}) copy-start(bf16[176,288]{1,0:T(8,128)(2,1)} %param.7) | copy-start | bytes 304132
  22.9 18.6 %copy-start.4 = (f32[1152,176]{0,1:T(8,128)}, f32[1152,176]{0,1:T(8,128)S(1)}, u32[]{:S(2)}) copy-start(f32[1152,176]{0,1:T(8,128)S(1)} %reshape.33) | copy-start | bytes 2433028
  23.2 31.3 %collective-permute-start.4 = (bf16[176,1152]{1,0:T(8,128)(2,1)S(1)}, bf16[176,1152]{1,0:T(8,128)(2,1)S(1)}, u32[]{:S(2)}, u32[]{:S(2)}) collective-permute-start(bf16[176,1152]{1,0:T(8,128)(2,1)S(1)} %bitcast_convert_fusion), channel_id=1, source_target_pairs={{0,508},{4,0},{8,4},{12,8},{16,12},{20,16},{24,20},{28,24},{32,28}... | collective-permute-start | bytes 1216520 | tf_op jit(solution)/shard_map/ppermute | solution.py:10
  42.3 46.8 %copy-start.2 = (f32[1152,176]{0,1:T(8,128)}, f32[1152,176]{0,1:T(8,128)S(1)}, u32[]{:S(2)}) copy-start(f32[1152,176]{0,1:T(8,128)S(1)} %reshape.32) | copy-start | bytes 2433028
  42.6 46.3 %collective-permute-start.2 = (bf16[176,1152]{1,0:T(8,128)(2,1)S(1)}, bf16[176,1152]{1,0:T(8,128)(2,1)S(1)}, u32[]{:S(2)}, u32[]{:S(2)}) collective-permute-start(bf16[176,1152]{1,0:T(8,128)(2,1)S(1)} %bitcast_convert_fusion.1), channel_id=1, source_target_pairs={{0,384},{4,388},{8,392},{12,396},{16,400},{20,404},{24,408},{28,41... | collective-permute-start | bytes 1216520 | tf_op jit(solution)/shard_map/ppermute | solution.py:10
  54.5 70.7 %collective-permute-start.5 = (bf16[176,1152]{1,0:T(8,128)(2,1)S(1)}, bf16[176,1152]{1,0:T(8,128)(2,1)S(1)}, u32[]{:S(2)}, u32[]{:S(2)}) collective-permute-start(bf16[176,1152]{1,0:T(8,128)(2,1)S(1)} %collective-permute-done.4), channel_id=1, source_target_pairs={{0,508},{4,0},{8,4},{12,8},{16,12},{20,16},{24,20},{28,24},{32,28}... | collective-permute-start | bytes 1216520 | tf_op jit(solution)/shard_map/ppermute | solution.py:10
  89.1 44.9 %collective-permute-start.3 = (bf16[176,1152]{1,0:T(8,128)(2,1)S(1)}, bf16[176,1152]{1,0:T(8,128)(2,1)S(1)}, u32[]{:S(2)}, u32[]{:S(2)}) collective-permute-start(bf16[176,1152]{1,0:T(8,128)(2,1)S(1)} %broadcast_select_fusion.1), channel_id=1, source_target_pairs={{0,256},{4,260},{8,264},{12,268},{16,272},{20,276},{24,280},{28,28... | collective-permute-start | bytes 1216520 | tf_op jit(solution)/shard_map/ppermute | solution.py:10
  125.1 18.6 %collective-permute-start.6 = (bf16[176,1152]{1,0:T(8,128)(2,1)S(1)}, bf16[176,1152]{1,0:T(8,128)(2,1)S(1)}, u32[]{:S(2)}, u32[]{:S(2)}) collective-permute-start(bf16[176,1152]{1,0:T(8,128)(2,1)S(1)} %collective-permute-done.5), channel_id=1, source_target_pairs={{0,508},{4,0},{8,4},{12,8},{16,12},{20,16},{24,20},{28,24},{32,28}... | collective-permute-start | bytes 1216520 | tf_op jit(solution)/shard_map/ppermute | solution.py:10
  134.0 12.4 %copy-start.6 = (bf16[176,1152]{1,0:T(8,128)(2,1)}, bf16[176,1152]{1,0:T(8,128)(2,1)S(1)}, u32[]{:S(2)}) copy-start(bf16[176,1152]{1,0:T(8,128)(2,1)S(1)} %broadcast_select_fusion.2) | copy-start | bytes 1216516
  143.9 1.2 copy-start
  147.2 13.6 %collective-permute-start = (bf16[176,1152]{1,0:T(8,128)(2,1)}, bf16[176,1152]{1,0:T(8,128)(2,1)}, u32[]{:S(2)}, u32[]{:S(2)}) collective-permute-start(bf16[176,1152]{1,0:T(8,128)(2,1)} %get-tuple-element.108), channel_id=1, source_target_pairs={{0,496},{4,500},{8,504},{12,508},{16,0},{20,4},{24,8},{28,12},{32,... | collective-permute-start | bytes 1216520 | tf_op jit(solution)/shard_map/while/body/eval_jaxpr/ppermute | solution.py:10
  149.1 29.1 %collective-permute-start.1 = (f32[176,1152]{1,0:T(8,128)}, f32[176,1152]{1,0:T(8,128)}, u32[]{:S(2)}, u32[]{:S(2)}) collective-permute-start(f32[176,1152]{1,0:T(8,128)} %get-tuple-element.109), channel_id=1, source_target_pairs={{0,496},{4,500},{8,504},{12,508},{16,0},{20,4},{24,8},{28,12},{32,... | collective-permute-start | bytes 2433032 | tf_op jit(solution)/shard_map/while/body/eval_jaxpr/ppermute | solution.py:10
  165.5 12.7 %copy-start.1 = (bf16[704,1152]{1,0:T(8,128)(2,1)S(1)}, bf16[704,1152]{1,0:T(8,128)(2,1)}, u32[]{:S(2)}) copy-start(bf16[704,1152]{1,0:T(8,128)(2,1)} %get-tuple-element.120) | copy-start | bytes 4866052 | tf_op jit(solution)/shard_map/while
  180.8 12.7 %collective-permute-start = (bf16[176,1152]{1,0:T(8,128)(2,1)}, bf16[176,1152]{1,0:T(8,128)(2,1)}, u32[]{:S(2)}, u32[]{:S(2)}) collective-permute-start(bf16[176,1152]{1,0:T(8,128)(2,1)} %get-tuple-element.108), channel_id=1, source_target_pairs={{0,496},{4,500},{8,504},{12,508},{16,0},{20,4},{24,8},{28,12},{32,... | collective-permute-start | bytes 1216520 | tf_op jit(solution)/shard_map/while/body/eval_jaxpr/ppermute | solution.py:10
  185.1 25.7 %collective-permute-start.1 = (f32[176,1152]{1,0:T(8,128)}, f32[176,1152]{1,0:T(8,128)}, u32[]{:S(2)}, u32[]{:S(2)}) collective-permute-start(f32[176,1152]{1,0:T(8,128)} %get-tuple-element.109), channel_id=1, source_target_pairs={{0,496},{4,500},{8,504},{12,508},{16,0},{20,4},{24,8},{28,12},{32,... | collective-permute-start | bytes 2433032 | tf_op jit(solution)/shard_map/while/body/eval_jaxpr/ppermute | solution.py:10
  198.1 12.7 %copy-start.1 = (bf16[704,1152]{1,0:T(8,128)(2,1)S(1)}, bf16[704,1152]{1,0:T(8,128)(2,1)}, u32[]{:S(2)}) copy-start(bf16[704,1152]{1,0:T(8,128)(2,1)} %get-tuple-element.120) | copy-start | bytes 4866052 | tf_op jit(solution)/shard_map/while
  213.4 13.2 %collective-permute-start = (bf16[176,1152]{1,0:T(8,128)(2,1)}, bf16[176,1152]{1,0:T(8,128)(2,1)}, u32[]{:S(2)}, u32[]{:S(2)}) collective-permute-start(bf16[176,1152]{1,0:T(8,128)(2,1)} %get-tuple-element.108), channel_id=1, source_target_pairs={{0,496},{4,500},{8,504},{12,508},{16,0},{20,4},{24,8},{28,12},{32,... | collective-permute-start | bytes 1216520 | tf_op jit(solution)/shard_map/while/body/eval_jaxpr/ppermute | solution.py:10
  220.2 23.9 %collective-permute-start.1 = (f32[176,1152]{1,0:T(8,128)}, f32[176,1152]{1,0:T(8,128)}, u32[]{:S(2)}, u32[]{:S(2)}) collective-permute-start(f32[176,1152]{1,0:T(8,128)} %get-tuple-element.109), channel_id=1, source_target_pairs={{0,496},{4,500},{8,504},{12,508},{16,0},{20,4},{24,8},{28,12},{32,... | collective-permute-start | bytes 2433032 | tf_op jit(solution)/shard_map/while/body/eval_jaxpr/ppermute | solution.py:10
  231.3 12.8 %copy-start.1 = (bf16[704,1152]{1,0:T(8,128)(2,1)S(1)}, bf16[704,1152]{1,0:T(8,128)(2,1)}, u32[]{:S(2)}) copy-start(bf16[704,1152]{1,0:T(8,128)(2,1)} %get-tuple-element.120) | copy-start | bytes 4866052 | tf_op jit(solution)/shard_map/while
  246.6 13.2 %collective-permute-start = (bf16[176,1152]{1,0:T(8,128)(2,1)}, bf16[176,1152]{1,0:T(8,128)(2,1)}, u32[]{:S(2)}, u32[]{:S(2)}) collective-permute-start(bf16[176,1152]{1,0:T(8,128)(2,1)} %get-tuple-element.108), channel_id=1, source_target_pairs={{0,496},{4,500},{8,504},{12,508},{16,0},{20,4},{24,8},{28,12},{32,... | collective-permute-start | bytes 1216520 | tf_op jit(solution)/shard_map/while/body/eval_jaxpr/ppermute | solution.py:10
  254.3 22.9 %collective-permute-start.1 = (f32[176,1152]{1,0:T(8,128)}, f32[176,1152]{1,0:T(8,128)}, u32[]{:S(2)}, u32[]{:S(2)}) collective-permute-start(f32[176,1152]{1,0:T(8,128)} %get-tuple-element.109), channel_id=1, source_target_pairs={{0,496},{4,500},{8,504},{12,508},{16,0},{20,4},{24,8},{28,12},{32,... | collective-permute-start | bytes 2433032 | tf_op jit(solution)/shard_map/while/body/eval_jaxpr/ppermute | solution.py:10
  264.5 12.7 %copy-start.1 = (bf16[704,1152]{1,0:T(8,128)(2,1)S(1)}, bf16[704,1152]{1,0:T(8,128)(2,1)}, u32[]{:S(2)}) copy-start(bf16[704,1152]{1,0:T(8,128)(2,1)} %get-tuple-element.120) | copy-start | bytes 4866052 | tf_op jit(solution)/shard_map/while
  279.8 12.9 %collective-permute-start = (bf16[176,1152]{1,0:T(8,128)(2,1)}, bf16[176,1152]{1,0:T(8,128)(2,1)}, u32[]{:S(2)}, u32[]{:S(2)}) collective-permute-start(bf16[176,1152]{1,0:T(8,128)(2,1)} %get-tuple-element.108), channel_id=1, source_target_pairs={{0,496},{4,500},{8,504},{12,508},{16,0},{20,4},{24,8},{28,12},{32,... | collective-permute-start | bytes 1216520 | tf_op jit(solution)/shard_map/while/body/eval_jaxpr/ppermute | solution.py:10
  287.5 22.0 %collective-permute-start.1 = (f32[176,1152]{1,0:T(8,128)}, f32[176,1152]{1,0:T(8,128)}, u32[]{:S(2)}, u32[]{:S(2)}) collective-permute-start(f32[176,1152]{1,0:T(8,128)} %get-tuple-element.109), channel_id=1, source_target_pairs={{0,496},{4,500},{8,504},{12,508},{16,0},{20,4},{24,8},{28,12},{32,... | collective-permute-start | bytes 2433032 | tf_op jit(solution)/shard_map/while/body/eval_jaxpr/ppermute | solution.py:10
  297.3 12.2 %copy-start.1 = (bf16[704,1152]{1,0:T(8,128)(2,1)S(1)}, bf16[704,1152]{1,0:T(8,128)(2,1)}, u32[]{:S(2)}) copy-start(bf16[704,1152]{1,0:T(8,128)(2,1)} %get-tuple-element.120) | copy-start | bytes 4866052 | tf_op jit(solution)/shard_map/while
  312.1 12.9 %collective-permute-start = (bf16[176,1152]{1,0:T(8,128)(2,1)}, bf16[176,1152]{1,0:T(8,128)(2,1)}, u32[]{:S(2)}, u32[]{:S(2)}) collective-permute-start(bf16[176,1152]{1,0:T(8,128)(2,1)} %get-tuple-element.108), channel_id=1, source_target_pairs={{0,496},{4,500},{8,504},{12,508},{16,0},{20,4},{24,8},{28,12},{32,... | collective-permute-start | bytes 1216520 | tf_op jit(solution)/shard_map/while/body/eval_jaxpr/ppermute | solution.py:10
  319.8 22.4 %collective-permute-start.1 = (f32[176,1152]{1,0:T(8,128)}, f32[176,1152]{1,0:T(8,128)}, u32[]{:S(2)}, u32[]{:S(2)}) collective-permute-start(f32[176,1152]{1,0:T(8,128)} %get-tuple-element.109), channel_id=1, source_target_pairs={{0,496},{4,500},{8,504},{12,508},{16,0},{20,4},{24,8},{28,12},{32,... | collective-permute-start | bytes 2433032 | tf_op jit(solution)/shard_map/while/body/eval_jaxpr/ppermute | solution.py:10
  329.6 12.6 %copy-start.1 = (bf16[704,1152]{1,0:T(8,128)(2,1)S(1)}, bf16[704,1152]{1,0:T(8,128)(2,1)}, u32[]{:S(2)}) copy-start(bf16[704,1152]{1,0:T(8,128)(2,1)} %get-tuple-element.120) | copy-start | bytes 4866052 | tf_op jit(solution)/shard_map/while
  344.8 11.5 %collective-permute-start = (bf16[176,1152]{1,0:T(8,128)(2,1)}, bf16[176,1152]{1,0:T(8,128)(2,1)}, u32[]{:S(2)}, u32[]{:S(2)}) collective-permute-start(bf16[176,1152]{1,0:T(8,128)(2,1)} %get-tuple-element.108), channel_id=1, source_target_pairs={{0,496},{4,500},{8,504},{12,508},{16,0},{20,4},{24,8},{28,12},{32,... | collective-permute-start | bytes 1216520 | tf_op jit(solution)/shard_map/while/body/eval_jaxpr/ppermute | solution.py:10
  351.2 23.3 %collective-permute-start.1 = (f32[176,1152]{1,0:T(8,128)}, f32[176,1152]{1,0:T(8,128)}, u32[]{:S(2)}, u32[]{:S(2)}) collective-permute-start(f32[176,1152]{1,0:T(8,128)} %get-tuple-element.109), channel_id=1, source_target_pairs={{0,496},{4,500},{8,504},{12,508},{16,0},{20,4},{24,8},{28,12},{32,... | collective-permute-start | bytes 2433032 | tf_op jit(solution)/shard_map/while/body/eval_jaxpr/ppermute | solution.py:10
  361.0 13.5 %copy-start.1 = (bf16[704,1152]{1,0:T(8,128)(2,1)S(1)}, bf16[704,1152]{1,0:T(8,128)(2,1)}, u32[]{:S(2)}) copy-start(bf16[704,1152]{1,0:T(8,128)(2,1)} %get-tuple-element.120) | copy-start | bytes 4866052 | tf_op jit(solution)/shard_map/while
  377.1 2.1 copy-start.7
  377.1 39.7 %collective-permute-start.7 = (f32[176,1152]{1,0:T(8,128)S(1)}, f32[176,1152]{1,0:T(8,128)S(1)}, u32[]{:S(2)}, u32[]{:S(2)}) collective-permute-start(f32[176,1152]{1,0:T(8,128)S(1)} %slice.16), channel_id=1, source_target_pairs={{0,4},{4,8},{8,12},{12,16},{16,20},{20,24},{24,28},{28,32},{32,36}... | collective-permute-start | bytes 2433032 | tf_op jit(solution)/shard_map/ppermute | solution.py:10
  379.2 70.3 %collective-permute-start.10 = (f32[176,1152]{1,0:T(8,128)S(1)}, f32[176,1152]{1,0:T(8,128)S(1)}, u32[]{:S(2)}, u32[]{:S(2)}) collective-permute-start(f32[176,1152]{1,0:T(8,128)S(1)} %copy-done.7), channel_id=1, source_target_pairs={{0,112},{4,116},{8,120},{12,124},{16,128},{20,132},{24,136},{28,14... | collective-permute-start | bytes 2433032 | tf_op jit(solution)/shard_map/ppermute | solution.py:10
  416.9 82.2 %collective-permute-start.8 = (f32[176,1152]{1,0:T(8,128)S(1)}, f32[176,1152]{1,0:T(8,128)S(1)}, u32[]{:S(2)}, u32[]{:S(2)}) collective-permute-start(f32[176,1152]{1,0:T(8,128)S(1)} %slice_add_fusion.1), channel_id=1, source_target_pairs={{0,4},{4,8},{8,12},{12,16},{16,20},{20,24},{24,28},{28,32},{32,36}... | collective-permute-start | bytes 2433032 | tf_op jit(solution)/shard_map/ppermute | solution.py:10
  449.5 51.8 %collective-permute-start.11 = (f32[176,1152]{1,0:T(8,128)S(1)}, f32[176,1152]{1,0:T(8,128)S(1)}, u32[]{:S(2)}, u32[]{:S(2)}) collective-permute-start(f32[176,1152]{1,0:T(8,128)S(1)} %collective-permute-done.10), channel_id=1, source_target_pairs={{0,128},{4,132},{8,136},{12,140},{16,144},{20,148},{24,152},{28,15... | collective-permute-start | bytes 2433032 | tf_op jit(solution)/shard_map/ppermute | solution.py:10
  499.2 76.8 %copy-start.5 = (f32[1152,176]{0,1:T(8,128)S(1)}, f32[1152,176]{0,1:T(8,128)}, u32[]{:S(2)}) copy-start(f32[1152,176]{0,1:T(8,128)} %copy-done.4) | copy-start | bytes 2433028
  499.2 76.8 %collective-permute-start.9 = (f32[176,1152]{1,0:T(8,128)S(1)}, f32[176,1152]{1,0:T(8,128)S(1)}, u32[]{:S(2)}, u32[]{:S(2)}) collective-permute-start(f32[176,1152]{1,0:T(8,128)S(1)} %slice_add_fusion), channel_id=1, source_target_pairs={{0,4},{4,8},{8,12},{12,16},{16,20},{20,24},{24,28},{28,32},{32,36}... | collective-permute-start | bytes 2433032 | tf_op jit(solution)/shard_map/ppermute | solution.py:10
  502.3 77.8 %collective-permute-start.12 = (f32[176,1152]{1,0:T(8,128)}, f32[176,1152]{1,0:T(8,128)}, u32[]{:S(2)}, u32[]{:S(2)}) collective-permute-start(f32[176,1152]{1,0:T(8,128)} %broadcast_select_fusion), channel_id=1, source_target_pairs={{0,256},{4,260},{8,264},{12,268},{16,272},{20,276},{24,280},{28,28... | collective-permute-start | bytes 2433032 | tf_op jit(solution)/shard_map/ppermute | solution.py:10
  577.5 2.7 copy-start.3
  580.1 169.0 %reduce-scatter.9.cloned.1.call-start = ((), (), s32[]{:S(2)}) async-start(), calls=%async_computation.3 | async-start | bytes 1474560
Sparse Core Ops, SparseCore 0:
  580.2 117.8 reduce-scatter.6
  701.6 47.5 reduce-scatter.8
where the time goes:
time: 760 us; the launch traced here: 758 us
  waiting for transfers between devices  509 us (67%)
  starting transfers between devices  124 us (16%)
  matrix products  55.7 us (7%)
  blocking collectives  23.9 us (3%)
  local copies, waits for them, and re-layouts  22.2 us (3%)
  between operations  15.7 us (2%)
    ppermute x25, waiting for transfers between devices, shifted_2(): return lax.ppermute(value, axis, pairs)  346 us
    unnamed x4, waiting for transfers between devices  163 us
    ppermute x25, starting transfers between devices, shifted_2(): return lax.ppermute(value, axis, pairs)  124 us
    dot_general x8, matrix products, pair_terms(): lax.dot_general(image_rows, text_rows, (((1,), (1,)), ((), ())), preferre...  20.6 us
    dot_general x8, matrix products, pair_terms(): lax.dot_general(pair_grad, image_rows, (((0,), (0,)), ((), ())), preferre...  19.5 us
    dot_general x8, matrix products, pair_terms(): to_image = jnp.dot(pair_grad, text_rows, preferred_element_type=jnp.float32)  15.7 us
  transfers between devices with their start and end apart: 27, of which 23 were waited for; matrix products, arithmetic and copies ran while one was open for 8% of the time, Pallas kernels for 0%

commit v1 on v0

v1 whole, which is shorter than its diff:
```python
import jax
import jax.numpy as jnp
from jax import lax
from jax.experimental import pallas as pl
from jax.experimental.pallas import tpu as pltpu
from jax.sharding import PartitionSpec as P

MESH = pl.DeviceIdType.MESH
BF = jnp.bfloat16
F32 = jnp.float32
NX, NY, NZ = 4, 4, 16
SHARD = 48
IMG_Z = (0, 1, -1, 2)
TXT_Z = (0, 8, 4, 12)
CHUNK = 256


def coords():
    dp, t = lax.axis_index("dp"), lax.axis_index("tensor")
    return (t // 2) * 2 + lax.rem(dp, 2), lax.rem(dp // 2, NY), dp // (2 * NY), lax.rem(t, 2)


def device(x, y, z, c):
    x, y, z = lax.rem(x + 2 * NX, NX), lax.rem(y + 2 * NY, NY), lax.rem(z + 2 * NZ, NZ)
    return (z * (2 * NY) + y * 2 + lax.rem(x, 2), (x // 2) * 2 + lax.rem(c, 2))


def at(slot, count=1):
    return pl.ds(slot * SHARD, count * SHARD)


def img_slot(g, d):
    return g * 4 + d


def txt_slot(g, core, d):
    return g * 8 + core * 4 + d


def kernel(
    scale_ref, bias_ref, img_in, txt_in, img_out, txt_out,
    block, raw, img, txt, img_grad, txt_grad,
    core_send, core_got, x_send, x_got, y_send, y_got, z_send, z_got, back,
    in_sem, gs, gr, rs, rr,
):
    x, y, z, c = coords()
    dp, t = lax.axis_index("dp"), lax.axis_index("tensor")
    quarter = block.shape[2]
    rows_in = img_in.shape[0]
    mirror = 1 - 2 * c

    loads = [
        pltpu.make_async_copy(ref, block.at[e, pl.ds(0, rows_in)], in_sem.at[e])
        for e, ref in enumerate((img_in, txt_in))
    ]
    for load in loads:
        load.start()
    for e in range(2):
        block[e, rows_in:, :] = jnp.zeros((block.shape[1] - rows_in, quarter), BF)

    peers = [(x, y, z + d, c) for d in (1, -1, 2, -2, 4, 8, 12)]
    peers += [(x, y + d, z, c) for d in (1, 2, 3)] + [(x + d, y, z, c) for d in (1, 2, 3)]
    peers += [(x, y, z, c + 1), (x + 2, y, z, c + 1)]
    barrier = pltpu.get_barrier_semaphore()
    for peer in peers:
        pl.semaphore_signal(barrier, inc=1, device_id=device(*peer), device_id_type=MESH)
    pl.semaphore_wait(barrier, len(peers))

    sent = []

    def go(copy):
        copy.start()
        sent.append(copy)

    def remote(src, dst, sems, index, to):
        return pltpu.make_async_remote_copy(
            src_ref=src, dst_ref=dst, send_sem=sems[0].at[index], recv_sem=sems[1].at[index],
            device_id=to, device_id_type=MESH,
        )

    gather, reduce = (gs, gr), (rs, rr)

    def swap(e, j):
        to = lax.rem(t + j, 4)
        rows = pl.ds(pl.multiple_of(to * SHARD, SHARD), SHARD)
        return remote(block.at[e, rows], raw.at[e, t], gather, e * 3 + j - 1, (dp, to))

    for e in (1, 0):
        loads[e].wait()
        for j in (2, 3, 1):
            go(swap(e, j))
        raw[e, t] = block[e, pl.ds(pl.multiple_of(t * SHARD, SHARD), SHARD), :]

    def unit(e):
        rows = jnp.concatenate([raw[e, q].astype(F32) for q in range(4)], axis=1)
        norm = jnp.sqrt(jnp.sum(rows * rows, axis=1, keepdims=True) + 1e-06)
        return rows / norm, norm

    def txt_z(g):
        to = device(x, y, z + TXT_Z[g], c)
        return remote(txt.at[at(0)], txt.at[at(txt_slot(g, 0, 0))], gather, 5 + g, to)

    def txt_x(g, d):
        to = device(x + d, y, z, c)
        return remote(txt.at[at(txt_slot(g, 0, 0))], txt.at[at(txt_slot(g, 0, d))], gather, 8 + g * 3 + d, to)

    def txt_core(g, d):
        to = device(x, y, z, c + 1)
        return remote(txt.at[at(txt_slot(g, 0, d))], txt.at[at(txt_slot(g, 1, d))], gather, 21 + g * 4 + d, to)

    def img_z(g):
        to = device(x, y, z + IMG_Z[g] * mirror, c)
        return remote(img.at[at(0)], img.at[at(img_slot(g, 0))], gather, 36 + g, to)

    def img_y(g, d):
        to = device(x, y + d, z, c)
        return remote(img.at[at(img_slot(g, 0))], img.at[at(img_slot(g, d))], gather, 39 + g * 3 + d, to)

    for j in (1, 2, 3):
        swap(1, j).wait_recv()
    txt[at(0), :] = unit(1)[0].astype(BF)
    for g in (1, 2, 3):
        go(txt_z(g))
    for d in (2, 1, 3):
        go(txt_x(0, d))
    go(txt_core(0, 0))
    for j in (1, 2, 3):
        swap(0, j).wait_recv()
    img[at(0), :] = unit(0)[0].astype(BF)
    for g in (3, 1, 2):
        go(img_z(g))
    for d in (2, 1, 3):
        go(img_y(0, d))

    img_grad[...] = jnp.zeros_like(img_grad)
    txt_grad[...] = jnp.zeros_like(txt_grad)
    scale = jnp.exp(jnp.full((1, 1), scale_ref[0], F32))
    bias = bias_ref[0]

    def forward_x(g):
        txt_z(g).wait_recv()
        go(txt_core(g, 0))
        for d in (2, 1, 3):
            go(txt_x(g, d))

    def forward_core(g):
        for d in (1, 3, 2):
            txt_x(g, d).wait_recv()
            go(txt_core(g, d))

    def got_core(g):
        for d in range(4):
            txt_core(g, d).wait_recv()

    def pairs(g):
        here = at(txt_slot(g, 0, 0), 8)

        def step(k, carry):
            there = pl.ds(pl.multiple_of(k * CHUNK, CHUNK), CHUNK)
            scores = lax.dot_general(
                img[there, :], txt[here, :], (((1,), (1,)), ((), ())), preferred_element_type=F32
            )
            part = jax.nn.sigmoid(scale * scores + bias).astype(BF)
            img_grad[there, :] += jnp.dot(part, txt[here, :], preferred_element_type=F32)
            txt_grad[here, :] += lax.dot_general(
                part, img[there, :], (((0,), (0,)), ((), ())), preferred_element_type=F32
            )
            return carry

        lax.fori_loop(0, img.shape[0] // CHUNK, step, 0)

    def cut_core(g):
        to = device(x, y, z, c + 1)
        return remote(core_send.at[g], core_got.at[g], reduce, g, to)

    def cut_x(g, d):
        to = device(x - d, y, z, c)
        return remote(x_send.at[g, d - 1], x_got.at[g, d - 1], reduce, 3 + g * 3 + d, to)

    def cut_y(g, d):
        to = device(x, y - d, z, c)
        return remote(y_send.at[g, d - 1], y_got.at[g, d - 1], reduce, 15 + g * 3 + d, to)

    def cut_z(e, g):
        to = device(x, y, z - (TXT_Z[g] if e else IMG_Z[g] * mirror), c)
        return remote(z_send.at[e, g - 1], z_got.at[e, g - 1], reduce, 27 + e * 3 + g, to)

    def give_core(g):
        core_send[g] = txt_grad[at(txt_slot(g, 1, 0), 4), :].astype(BF)
        go(cut_core(g))

    def give_x(g):
        cut_core(g).wait_recv()
        for d in (2, 1, 3):
            mine = txt_grad[at(txt_slot(g, 0, d)), :]
            x_send[g, d - 1] = (mine + core_got[g, at(d), :].astype(F32)).astype(BF)
            go(cut_x(g, d))
        return None

    def txt_total(g):
        total = txt_grad[at(txt_slot(g, 0, 0)), :] + core_got[g, at(0), :].astype(F32)
        for d in (1, 3, 2):
            cut_x(g, d).wait_recv()
            total += x_got[g, d - 1].astype(F32)
        return total

    def img_total(g):
        total = img_grad[at(img_slot(g, 0)), :]
        for d in (1, 3, 2):
            cut_y(g, d).wait_recv()
            total += y_got[g, d - 1].astype(F32)
        return total

    def give_z(e, g):
        z_send[e, g - 1] = (txt_total(g) if e else img_total(g)).astype(BF)
        go(cut_z(e, g))

    def swap_back(e, j):
        to = lax.rem(t + j, 4)
        out = (img_out, txt_out)[e]
        rows = pl.ds(pl.multiple_of(t * SHARD, SHARD), SHARD)
        return remote(back.at[e, to], out.at[rows], reduce, 34 + e * 3 + j - 1, (dp, to))

    def finish(e):
        total = txt_total(0) if e else img_total(0)
        for g in (1, 2, 3):
            cut_z(e, g).wait_recv()
            total += z_got[e, g - 1].astype(F32)
        rows, norm = unit(e)
        own = (txt, img)[e][at(0), :].astype(F32)
        grad = scale * (total - own)
        inner = jnp.sum(rows * grad, axis=1, keepdims=True)
        grad = ((grad - rows * inner) / norm).astype(BF)
        for q in range(4):
            back[e, q] = grad[:, q * quarter : (q + 1) * quarter]
        for j in (2, 3, 1):
            go(swap_back(e, j))
        keep = pltpu.make_async_copy(
            back.at[e, t], (img_out, txt_out)[e].at[pl.ds(pl.multiple_of(t * SHARD, SHARD), SHARD)], in_sem.at[e]
        )
        keep.start()
        return keep

    forward_core(0)
    for g in (1, 2, 3):
        img_z(g).wait_recv()
        for d in (2, 1, 3):
            go(img_y(g, d))
    for g in range(4):
        for d in (1, 2, 3):
            img_y(g, d).wait_recv()
    got_core(0)
    pairs(0)
    give_core(0)
    forward_x(2)
    forward_x(3)
    forward_core(2)
    forward_core(3)
    got_core(2)
    pairs(2)
    give_core(2)
    give_x(0)
    forward_x(1)
    got_core(3)
    pairs(3)
    give_core(3)
    give_x(2)
    forward_core(1)
    give_z(1, 2)
    give_x(3)
    got_core(1)
    pairs(1)
    give_core(1)
    for g in (3, 1, 2, 0):
        for d in (2, 1, 3):
            y_send[g, d - 1] = img_grad[at(img_slot(g, d)), :].astype(BF)
            go(cut_y(g, d))
    give_x(1)
    give_z(1, 3)
    for g in (3, 1, 2):
        give_z(0, g)
    give_z(1, 1)
    keep = [finish(0), finish(1)]
    for e in range(2):
        for j in (1, 2, 3):
            swap_back(e, j).wait_recv()
        keep[e].wait()
    for copy in sent:
        copy.wait_send()


def body(image_embed, text_embed, log_scale, logit_bias):
    rows, quarter = image_embed.shape
    width = 4 * quarter
    padded = 4 * SHARD
    vmem = pltpu.VMEM
    outs = pl.pallas_call(
        kernel,
        out_shape=[jax.ShapeDtypeStruct((padded, quarter), BF)] * 2,
        in_specs=[pl.BlockSpec(memory_space=pltpu.SMEM)] * 2 + [pl.BlockSpec(memory_space=pl.ANY)] * 2,
        out_specs=[pl.BlockSpec(memory_space=pl.ANY)] * 2,
        scratch_shapes=[
            vmem((2, padded, quarter), BF),
            vmem((2, 4, SHARD, quarter), BF),
            vmem((16 * SHARD, width), BF),
            vmem((32 * SHARD, width), BF),
            vmem((16 * SHARD, width), F32),
            vmem((32 * SHARD, width), F32),
            vmem((4, 4 * SHARD, width), BF),
            vmem((4, 4 * SHARD, width), BF),
            vmem((4, 3, SHARD, width), BF),
            vmem((4, 3, SHARD, width), BF),
            vmem((4, 3, SHARD, width), BF),
            vmem((4, 3, SHARD, width), BF),
            vmem((2, 3, SHARD, width), BF),
            vmem((2, 3, SHARD, width), BF),
            vmem((2, 4, SHARD, quarter), BF),
            pltpu.SemaphoreType.DMA((2,)),
            pltpu.SemaphoreType.DMA((52,)),
            pltpu.SemaphoreType.DMA((52,)),
            pltpu.SemaphoreType.DMA((40,)),
            pltpu.SemaphoreType.DMA((40,)),
        ],
        compiler_params=pltpu.CompilerParams(
            collective_id=0, has_side_effects=True, vmem_limit_bytes=56 * 2**20
        ),
    )(log_scale, logit_bias, image_embed, text_embed)
    return tuple(out[:rows].astype(F32) for out in outs)


def solution(mesh):
    placed = (P("dp", "tensor"), P("dp", "tensor"), P(), P())
    return jax.shard_map(
        body,
        mesh=mesh,
        in_specs=placed,
        out_specs=(P("dp", "tensor"), P("dp", "tensor")),
        check_vma=False,
    )
```

time: 760 us -> 143 us (0.19)
  the two profiles are of different devices: /device:TPU:1 before, /device:TPU:33 now
where the time goes in v1:
time: 143 us
  Pallas kernels  139 us (97%)
  between operations  1.93 us (1%)
  other arithmetic  1.8 us (1%)
    pallas_call x1, Pallas kernels, body(): pl.pallas_call(kernel, out_shape=[jax.ShapeDtypeStruct((padded, quarter),...  139 us

profile of v1, /device:TPU:33, one launch (start us, length us, event | category | flops | bytes accessed | tf_op | source)
XLA Modules:
  0.0 142.9 jit_solution(9614774034725730032)
XLA Ops:
  1.9 139.1 %shard_map.59 = (bf16[192,288]{1,0:T(8,128)(2,1)}, bf16[192,288]{1,0:T(8,128)(2,1)}) custom-call(f32[1]{0:T(128)S(6)} %copy.6.scale_ref, f32[1]{0:T(128)S(6)} %copy.7.bias_ref, bf16[176,288]{1,0:T(8,128)(2,1)} %img_in.1, bf16[176,288]{1,0:T(8,128)(2,1)} %txt_in.1), custom_call_target="tpu_custom_call" | custom-call | tf_op jit(solution)/shard_map/pallas_call | solution.py:297
  141.1 1.8 %slice_convert_fusion = (f32[176,288]{1,0:T(8,128)}, f32[176,288]{1,0:T(8,128)}) fusion(bf16[192,288]{1,0:T(8,128)(2,1)} %get-tuple-element.5, bf16[192,288]{1,0:T(8,128)(2,1)} %get-tuple-element.4), kind=kLoop, calls=%fused_computation | loop fusion | flops 101376 | bytes 608256 | tf_op jit(solution)/shard_map/convert_element_type | solution.py:328

commit v2 on v1

--- a/solution.py
+++ b/solution.py
@@ -30,7 +30,7 @@
 
 
 def img_slot(g, d):
-    return g * 4 + d
+    return (3 - g) * 4 + d
 
 
 def txt_slot(g, core, d):
@@ -85,7 +85,7 @@
         rows = pl.ds(pl.multiple_of(to * SHARD, SHARD), SHARD)
         return remote(block.at[e, rows], raw.at[e, t], gather, e * 3 + j - 1, (dp, to))
 
-    for e in (1, 0):
+    for e in (0, 1):
         loads[e].wait()
         for j in (2, 3, 1):
             go(swap(e, j))
@@ -110,27 +110,28 @@
 
     def img_z(g):
         to = device(x, y, z + IMG_Z[g] * mirror, c)
-        return remote(img.at[at(0)], img.at[at(img_slot(g, 0))], gather, 36 + g, to)
+        return remote(img.at[at(img_slot(0, 0))], img.at[at(img_slot(g, 0))], gather, 36 + g, to)
 
     def img_y(g, d):
         to = device(x, y + d, z, c)
         return remote(img.at[at(img_slot(g, 0))], img.at[at(img_slot(g, d))], gather, 39 + g * 3 + d, to)
 
-    for j in (1, 2, 3):
-        swap(1, j).wait_recv()
-    txt[at(0), :] = unit(1)[0].astype(BF)
-    for g in (1, 2, 3):
-        go(txt_z(g))
-    for d in (2, 1, 3):
-        go(txt_x(0, d))
-    go(txt_core(0, 0))
-    for j in (1, 2, 3):
+    own_img, own_txt = at(img_slot(0, 0)), at(txt_slot(0, 0, 0))
+    for j in (1, 3, 2):
         swap(0, j).wait_recv()
-    img[at(0), :] = unit(0)[0].astype(BF)
+    img[own_img, :] = unit(0)[0].astype(BF)
     for g in (3, 1, 2):
         go(img_z(g))
     for d in (2, 1, 3):
         go(img_y(0, d))
+    for j in (1, 3, 2):
+        swap(1, j).wait_recv()
+    txt[own_txt, :] = unit(1)[0].astype(BF)
+    for g in (2, 3):
+        txt_z(g).start()
+    for d in (2, 1, 3):
+        go(txt_x(0, d))
+    go(txt_core(0, 0))
 
     img_grad[...] = jnp.zeros_like(img_grad)
     txt_grad[...] = jnp.zeros_like(txt_grad)
@@ -152,19 +153,21 @@
         for d in range(4):
             txt_core(g, d).wait_recv()
 
+    def pairs_chunk(g, k):
+        here = at(txt_slot(g, 0, 0), 8)
+        there = pl.ds(k * CHUNK if isinstance(k, int) else pl.multiple_of(k * CHUNK, CHUNK), CHUNK)
+        scores = lax.dot_general(
+            img[there, :], txt[here, :], (((1,), (1,)), ((), ())), preferred_element_type=F32
+        )
+        part = jax.nn.sigmoid(scale * scores + bias).astype(BF)
+        img_grad[there, :] += jnp.dot(part, txt[here, :], preferred_element_type=F32)
+        txt_grad[here, :] += lax.dot_general(
+            part, img[there, :], (((0,), (0,)), ((), ())), preferred_element_type=F32
+        )
+
     def pairs(g):
-        here = at(txt_slot(g, 0, 0), 8)
-
         def step(k, carry):
-            there = pl.ds(pl.multiple_of(k * CHUNK, CHUNK), CHUNK)
-            scores = lax.dot_general(
-                img[there, :], txt[here, :], (((1,), (1,)), ((), ())), preferred_element_type=F32
-            )
-            part = jax.nn.sigmoid(scale * scores + bias).astype(BF)
-            img_grad[there, :] += jnp.dot(part, txt[here, :], preferred_element_type=F32)
-            txt_grad[here, :] += lax.dot_general(
-                part, img[there, :], (((0,), (0,)), ((), ())), preferred_element_type=F32
-            )
+            pairs_chunk(g, k)
             return carry
 
         lax.fori_loop(0, img.shape[0] // CHUNK, step, 0)
@@ -184,6 +187,10 @@
     def cut_z(e, g):
         to = device(x, y, z - (TXT_Z[g] if e else IMG_Z[g] * mirror), c)
         return remote(z_send.at[e, g - 1], z_got.at[e, g - 1], reduce, 27 + e * 3 + g, to)
+
+    def give_y(g, d):
+        y_send[g, d - 1] = img_grad[at(img_slot(g, d)), :].astype(BF)
+        go(cut_y(g, d))
 
     def give_core(g):
         core_send[g] = txt_grad[at(txt_slot(g, 1, 0), 4), :].astype(BF)
@@ -227,7 +234,7 @@
             cut_z(e, g).wait_recv()
             total += z_got[e, g - 1].astype(F32)
         rows, norm = unit(e)
-        own = (txt, img)[e][at(0), :].astype(F32)
+        own = (txt[own_txt, :], img[own_img, :])[e].astype(F32)
         grad = scale * (total - own)
         inner = jnp.sum(rows * grad, axis=1, keepdims=True)
         grad = ((grad - rows * inner) / norm).astype(BF)
@@ -241,42 +248,48 @@
         keep.start()
         return keep
 
-    forward_core(0)
     for g in (1, 2, 3):
         img_z(g).wait_recv()
         for d in (2, 1, 3):
             go(img_y(g, d))
+    forward_core(0)
+    for g in (2, 3):
+        txt_z(g).wait_send()
+    go(txt_z(1))
+    forward_x(2)
+    forward_x(3)
     for g in range(4):
         for d in (1, 2, 3):
             img_y(g, d).wait_recv()
     got_core(0)
     pairs(0)
     give_core(0)
-    forward_x(2)
-    forward_x(3)
     forward_core(2)
-    forward_core(3)
+    give_x(0)
     got_core(2)
     pairs(2)
     give_core(2)
-    give_x(0)
+    forward_core(3)
     forward_x(1)
+    give_x(2)
     got_core(3)
     pairs(3)
     give_core(3)
-    give_x(2)
     forward_core(1)
     give_z(1, 2)
     give_x(3)
     got_core(1)
-    pairs(1)
-    give_core(1)
-    for g in (3, 1, 2, 0):
-        for d in (2, 1, 3):
-            y_send[g, d - 1] = img_grad[at(img_slot(g, d)), :].astype(BF)
-            go(cut_y(g, d))
+    done = 0
+    for k in range(img.shape[0] // CHUNK):
+        pairs_chunk(1, k)
+        if (k + 1) * CHUNK == img.shape[0]:
+            give_core(1)
+        for slot in range(done, (k + 1) * CHUNK // SHARD):
+            if slot % 4:
+                give_y(3 - slot // 4, slot % 4)
+            done = slot + 1
+    give_z(1, 3)
     give_x(1)
-    give_z(1, 3)
     for g in (3, 1, 2):
         give_z(0, g)
     give_z(1, 1)

time: 143 us -> 115 us (0.80)
  the two profiles are of different devices: /device:TPU:33 before, /device:TPU:1 now
where the time goes in v2:
time: 115 us
  Pallas kernels  111 us (97%)
  between operations  1.93 us (2%)
  other arithmetic  1.8 us (2%)
    pallas_call x1, Pallas kernels, body(): pl.pallas_call(kernel, out_shape=[jax.ShapeDtypeStruct((padded, quarter),...  111 us

profile of v2, /device:TPU:1, one launch (start us, length us, event | category | flops | bytes accessed | tf_op | source)
XLA Modules:
  0.0 115.0 jit_solution(9024633071560687604)
XLA Ops:
  1.9 111.3 %shard_map.59 = (bf16[192,288]{1,0:T(8,128)(2,1)}, bf16[192,288]{1,0:T(8,128)(2,1)}) custom-call(f32[1]{0:T(128)S(6)} %copy.6.scale_ref, f32[1]{0:T(128)S(6)} %copy.7.bias_ref, bf16[176,288]{1,0:T(8,128)(2,1)} %img_in.1, bf16[176,288]{1,0:T(8,128)(2,1)} %txt_in.1), custom_call_target="tpu_custom_call" | custom-call | tf_op jit(solution)/shard_map/pallas_call | solution.py:310
  113.2 1.8 %slice_convert_fusion = (f32[176,288]{1,0:T(8,128)}, f32[176,288]{1,0:T(8,128)}) fusion(bf16[192,288]{1,0:T(8,128)(2,1)} %get-tuple-element.5, bf16[192,288]{1,0:T(8,128)(2,1)} %get-tuple-element.4), kind=kLoop, calls=%fused_computation | loop fusion | flops 101376 | bytes 608256 | tf_op jit(solution)/shard_map/convert_element_type | solution.py:341

commit v3 on v2

--- a/solution.py
+++ b/solution.py
@@ -12,7 +12,8 @@
 SHARD = 48
 IMG_Z = (0, 1, -1, 2)
 TXT_Z = (0, 8, 4, 12)
-CHUNK = 256
+FIRST = 2
+HALF = 640
 
 
 def coords():
@@ -38,8 +39,8 @@
 
 
 def kernel(
-    scale_ref, bias_ref, img_in, txt_in, img_out, txt_out,
-    block, raw, img, txt, img_grad, txt_grad,
+    scale_in, bias_in, img_in, txt_in, img_out, txt_out,
+    scale_ref, bias_ref, block, raw, img, txt, img_grad, txt_grad,
     core_send, core_got, x_send, x_got, y_send, y_got, z_send, z_got, back,
     in_sem, gs, gr, rs, rr,
 ):
@@ -53,6 +54,8 @@
         pltpu.make_async_copy(ref, block.at[e, pl.ds(0, rows_in)], in_sem.at[e])
         for e, ref in enumerate((img_in, txt_in))
     ]
+    loads.append(pltpu.make_async_copy(scale_in, scale_ref, in_sem.at[2]))
+    loads.append(pltpu.make_async_copy(bias_in, bias_ref, in_sem.at[3]))
     for load in loads:
         load.start()
     for e in range(2):
@@ -99,6 +102,12 @@
     def txt_z(g):
         to = device(x, y, z + TXT_Z[g], c)
         return remote(txt.at[at(0)], txt.at[at(txt_slot(g, 0, 0))], gather, 5 + g, to)
+
+    def txt_far(h):
+        lanes = (pl.ds(0, HALF), pl.ds(HALF, txt.shape[1] - HALF))[h]
+        to = device(x, y, z + (4, -4)[h], c)
+        src, dst = txt.at[at(txt_slot(2 + h, 0, 0)), lanes], txt.at[at(txt_slot(1, 0, 0)), lanes]
+        return remote(src, dst, gather, (6, 52)[h], to)
 
     def txt_x(g, d):
         to = device(x + d, y, z, c)
@@ -128,18 +137,23 @@
         swap(1, j).wait_recv()
     txt[own_txt, :] = unit(1)[0].astype(BF)
     for g in (2, 3):
-        txt_z(g).start()
+        go(txt_z(g))
     for d in (2, 1, 3):
         go(txt_x(0, d))
     go(txt_core(0, 0))
 
-    img_grad[...] = jnp.zeros_like(img_grad)
-    txt_grad[...] = jnp.zeros_like(txt_grad)
+    for load in loads[2:]:
+        load.wait()
     scale = jnp.exp(jnp.full((1, 1), scale_ref[0], F32))
     bias = bias_ref[0]
 
     def forward_x(g):
-        txt_z(g).wait_recv()
+        if g == 1:
+            txt_far(0).wait_recv()
+            txt_far(1).wait_recv()
+        else:
+            txt_z(g).wait_recv()
+            go(txt_far(g - 2))
         go(txt_core(g, 0))
         for d in (2, 1, 3):
             go(txt_x(g, d))
@@ -153,24 +167,22 @@
         for d in range(4):
             txt_core(g, d).wait_recv()
 
-    def pairs_chunk(g, k):
-        here = at(txt_slot(g, 0, 0), 8)
-        there = pl.ds(k * CHUNK if isinstance(k, int) else pl.multiple_of(k * CHUNK, CHUNK), CHUNK)
+    def pairs(g, first=0, count=16):
+        here, there = at(txt_slot(g, 0, 0), 8), at(first, count)
         scores = lax.dot_general(
             img[there, :], txt[here, :], (((1,), (1,)), ((), ())), preferred_element_type=F32
         )
         part = jax.nn.sigmoid(scale * scores + bias).astype(BF)
-        img_grad[there, :] += jnp.dot(part, txt[here, :], preferred_element_type=F32)
-        txt_grad[here, :] += lax.dot_general(
-            part, img[there, :], (((0,), (0,)), ((), ())), preferred_element_type=F32
-        )
-
-    def pairs(g):
-        def step(k, carry):
-            pairs_chunk(g, k)
-            return carry
-
-        lax.fori_loop(0, img.shape[0] // CHUNK, step, 0)
+        to_img = jnp.dot(part, txt[here, :], preferred_element_type=F32)
+        if g == FIRST:
+            img_grad[there, :] = to_img
+        else:
+            img_grad[there, :] += to_img
+        to_txt = lax.dot_general(part, img[there, :], (((0,), (0,)), ((), ())), preferred_element_type=F32)
+        if first == 0:
+            txt_grad[here, :] = to_txt
+        else:
+            txt_grad[here, :] += to_txt
 
     def cut_core(g):
         to = device(x, y, z, c + 1)
@@ -253,46 +265,39 @@
         for d in (2, 1, 3):
             go(img_y(g, d))
     forward_core(0)
-    for g in (2, 3):
-        txt_z(g).wait_send()
-    go(txt_z(1))
     forward_x(2)
     forward_x(3)
     for g in range(4):
         for d in (1, 2, 3):
             img_y(g, d).wait_recv()
-    got_core(0)
-    pairs(0)
-    give_core(0)
+    forward_x(1)
     forward_core(2)
-    give_x(0)
     got_core(2)
     pairs(2)
     give_core(2)
     forward_core(3)
-    forward_x(1)
-    give_x(2)
     got_core(3)
     pairs(3)
     give_core(3)
+    give_x(2)
     forward_core(1)
-    give_z(1, 2)
     give_x(3)
     got_core(1)
-    done = 0
-    for k in range(img.shape[0] // CHUNK):
-        pairs_chunk(1, k)
-        if (k + 1) * CHUNK == img.shape[0]:
-            give_core(1)
-        for slot in range(done, (k + 1) * CHUNK // SHARD):
+    pairs(1)
+    give_core(1)
+    got_core(0)
+    for first in (0, 8):
+        pairs(0, first, 8)
+        give_x(1) if first == 0 else give_core(0)
+        for slot in range(first, first + 8):
             if slot % 4:
                 give_y(3 - slot // 4, slot % 4)
-            done = slot + 1
+    give_z(1, 2)
+    give_x(0)
     give_z(1, 3)
-    give_x(1)
-    for g in (3, 1, 2):
+    give_z(1, 1)
+    for g in (3, 2, 1):
         give_z(0, g)
-    give_z(1, 1)
     keep = [finish(0), finish(1)]
     for e in range(2):
         for j in (1, 2, 3):
@@ -310,9 +315,11 @@
     outs = pl.pallas_call(
         kernel,
         out_shape=[jax.ShapeDtypeStruct((padded, quarter), BF)] * 2,
-        in_specs=[pl.BlockSpec(memory_space=pltpu.SMEM)] * 2 + [pl.BlockSpec(memory_space=pl.ANY)] * 2,
+        in_specs=[pl.BlockSpec(memory_space=pl.ANY)] * 4,
         out_specs=[pl.BlockSpec(memory_space=pl.ANY)] * 2,
         scratch_shapes=[
+            pltpu.SMEM((1,), F32),
+            pltpu.SMEM((1,), F32),
             vmem((2, padded, quarter), BF),
             vmem((2, 4, SHARD, quarter), BF),
             vmem((16 * SHARD, width), BF),
@@ -328,9 +335,9 @@
             vmem((2, 3, SHARD, width), BF),
             vmem((2, 3, SHARD, width), BF),
             vmem((2, 4, SHARD, quarter), BF),
-            pltpu.SemaphoreType.DMA((2,)),
-            pltpu.SemaphoreType.DMA((52,)),
-            pltpu.SemaphoreType.DMA((52,)),
+            pltpu.SemaphoreType.DMA((4,)),
+            pltpu.SemaphoreType.DMA((53,)),
+            pltpu.SemaphoreType.DMA((53,)),
             pltpu.SemaphoreType.DMA((40,)),
             pltpu.SemaphoreType.DMA((40,)),
         ],

time: 115 us -> 105 us (0.913)
  Pallas kernels: 111 us -> 101 us
    pallas_call x1, Pallas kernels: 111 us -> 101 us  [body(): pl.pallas_call(kernel, out_shape=[jax.ShapeDtypeStruct((padded, quarter),...]
where the time goes in v3:
time: 105 us; the launch traced here: 104 us
  Pallas kernels  101 us (96%)
  between operations  1.93 us (2%)
  other arithmetic  1.8 us (2%)
    pallas_call x1, Pallas kernels, body(): pl.pallas_call(kernel, out_shape=[jax.ShapeDtypeStruct((padded, quarter),...  101 us

profile of v3, /device:TPU:1, one launch (start us, length us, event | category | flops | bytes accessed | tf_op | source)
XLA Modules:
  0.0 104.4 jit_solution(1825549127283556737)
XLA Ops:
  1.9 100.6 %shard_map.59 = (bf16[192,288]{1,0:T(8,128)(2,1)}, bf16[192,288]{1,0:T(8,128)(2,1)}) custom-call(f32[1]{0:T(128)S(6)} %copy.6.scale_in, f32[1]{0:T(128)S(6)} %copy.7.bias_in, bf16[176,288]{1,0:T(8,128)(2,1)} %img_in.1, bf16[176,288]{1,0:T(8,128)(2,1)} %txt_in.1), custom_call_target="tpu_custom_call" | custom-call | tf_op jit(solution)/shard_map/pallas_call | solution.py:315
  102.6 1.8 %slice_convert_fusion = (f32[176,288]{1,0:T(8,128)}, f32[176,288]{1,0:T(8,128)}) fusion(bf16[192,288]{1,0:T(8,128)(2,1)} %get-tuple-element.5, bf16[192,288]{1,0:T(8,128)(2,1)} %get-tuple-element.4), kind=kLoop, calls=%fused_computation | loop fusion | flops 101376 | bytes 608256 | tf_op jit(solution)/shard_map/convert_element_type | solution.py:348

commit v4 on v3

--- a/solution.py
+++ b/solution.py
@@ -40,7 +40,7 @@
 
 def kernel(
     scale_in, bias_in, img_in, txt_in, img_out, txt_out,
-    scale_ref, bias_ref, block, raw, img, txt, img_grad, txt_grad,
+    scale_ref, bias_ref, units, norms, block, raw, img, txt, img_grad, txt_grad,
     core_send, core_got, x_send, x_got, y_send, y_got, z_send, z_got, back,
     in_sem, gs, gr, rs, rr,
 ):
@@ -97,7 +97,9 @@
     def unit(e):
         rows = jnp.concatenate([raw[e, q].astype(F32) for q in range(4)], axis=1)
         norm = jnp.sqrt(jnp.sum(rows * rows, axis=1, keepdims=True) + 1e-06)
-        return rows / norm, norm
+        units[e] = rows / norm
+        norms[e] = jnp.broadcast_to(norm, norms.shape[1:])
+        return units[e].astype(BF)
 
     def txt_z(g):
         to = device(x, y, z + TXT_Z[g], c)
@@ -128,14 +130,14 @@
     own_img, own_txt = at(img_slot(0, 0)), at(txt_slot(0, 0, 0))
     for j in (1, 3, 2):
         swap(0, j).wait_recv()
-    img[own_img, :] = unit(0)[0].astype(BF)
+    img[own_img, :] = unit(0)
     for g in (3, 1, 2):
         go(img_z(g))
     for d in (2, 1, 3):
         go(img_y(0, d))
     for j in (1, 3, 2):
         swap(1, j).wait_recv()
-    txt[own_txt, :] = unit(1)[0].astype(BF)
+    txt[own_txt, :] = unit(1)
     for g in (2, 3):
         go(txt_z(g))
     for d in (2, 1, 3):
@@ -154,9 +156,9 @@
         else:
             txt_z(g).wait_recv()
             go(txt_far(g - 2))
-        go(txt_core(g, 0))
         for d in (2, 1, 3):
             go(txt_x(g, d))
+        go(txt_core(g, 0))
 
     def forward_core(g):
         for d in (1, 3, 2):
@@ -245,7 +247,7 @@
         for g in (1, 2, 3):
             cut_z(e, g).wait_recv()
             total += z_got[e, g - 1].astype(F32)
-        rows, norm = unit(e)
+        rows, norm = units[e], norms[e, :, :1]
         own = (txt[own_txt, :], img[own_img, :])[e].astype(F32)
         grad = scale * (total - own)
         inner = jnp.sum(rows * grad, axis=1, keepdims=True)
@@ -267,11 +269,11 @@
     forward_core(0)
     forward_x(2)
     forward_x(3)
+    forward_x(1)
+    forward_core(2)
     for g in range(4):
         for d in (1, 2, 3):
             img_y(g, d).wait_recv()
-    forward_x(1)
-    forward_core(2)
     got_core(2)
     pairs(2)
     give_core(2)
@@ -282,13 +284,16 @@
     give_x(2)
     forward_core(1)
     give_x(3)
+    got_core(0)
+    pairs(0, 0, 8)
     got_core(1)
     pairs(1)
     give_core(1)
-    got_core(0)
     for first in (0, 8):
-        pairs(0, first, 8)
-        give_x(1) if first == 0 else give_core(0)
+        if first:
+            give_x(1)
+            pairs(0, first, 8)
+            give_core(0)
         for slot in range(first, first + 8):
             if slot % 4:
                 give_y(3 - slot // 4, slot % 4)
@@ -320,6 +325,8 @@
         scratch_shapes=[
             pltpu.SMEM((1,), F32),
             pltpu.SMEM((1,), F32),
+            vmem((2, SHARD, width), F32),
+            vmem((2, SHARD, 128), F32),
             vmem((2, padded, quarter), BF),
             vmem((2, 4, SHARD, quarter), BF),
             vmem((16 * SHARD, width), BF),

time: 105 us -> 104 us (level)
  no operation moved by 1% of the time
where the time goes in v4:
time: 104 us
  Pallas kernels  100 us (96%)
  between operations  1.93 us (2%)
  other arithmetic  1.8 us (2%)
    pallas_call x1, Pallas kernels, body(): pl.pallas_call(kernel, out_shape=[jax.ShapeDtypeStruct((padded, quarter),...  100 us

profile of v4, /device:TPU:1, one launch (start us, length us, event | category | flops | bytes accessed | tf_op | source)
XLA Modules:
  0.0 104.0 jit_solution(8513615412415082875)
XLA Ops:
  1.9 100.2 %shard_map.59 = (bf16[192,288]{1,0:T(8,128)(2,1)}, bf16[192,288]{1,0:T(8,128)(2,1)}) custom-call(f32[1]{0:T(128)S(6)} %copy.6.scale_in, f32[1]{0:T(128)S(6)} %copy.7.bias_in, bf16[176,288]{1,0:T(8,128)(2,1)} %img_in.1, bf16[176,288]{1,0:T(8,128)(2,1)} %txt_in.1), custom_call_target="tpu_custom_call" | custom-call | tf_op jit(solution)/shard_map/pallas_call | solution.py:320
  102.2 1.8 %slice_convert_fusion = (f32[176,288]{1,0:T(8,128)}, f32[176,288]{1,0:T(8,128)}) fusion(bf16[192,288]{1,0:T(8,128)(2,1)} %get-tuple-element.5, bf16[192,288]{1,0:T(8,128)(2,1)} %get-tuple-element.4), kind=kLoop, calls=%fused_computation | loop fusion | flops 101376 | bytes 608256 | tf_op jit(solution)/shard_map/convert_element_type | solution.py:355

commit v5 on v4

--- a/solution.py
+++ b/solution.py
@@ -127,13 +127,24 @@
         to = device(x, y + d, z, c)
         return remote(img.at[at(img_slot(g, 0))], img.at[at(img_slot(g, d))], gather, 39 + g * 3 + d, to)
 
+    def img_far(g, h):
+        lanes = (pl.ds(0, HALF), pl.ds(HALF, img.shape[1] - HALF))[h]
+        to = device(x, y + (1, -1)[h], z, c)
+        src, dst = img.at[at(img_slot(g, (1, 3)[h])), lanes], img.at[at(img_slot(g, 2)), lanes]
+        return remote(src, dst, gather, (41 + g * 3, 53 + g)[h], to)
+
+    def forward_y(g):
+        for h, d in enumerate((1, 3)):
+            img_y(g, d).wait_recv()
+            go(img_far(g, h))
+
     own_img, own_txt = at(img_slot(0, 0)), at(txt_slot(0, 0, 0))
     for j in (1, 3, 2):
         swap(0, j).wait_recv()
     img[own_img, :] = unit(0)
     for g in (3, 1, 2):
         go(img_z(g))
-    for d in (2, 1, 3):
+    for d in (1, 3):
         go(img_y(0, d))
     for j in (1, 3, 2):
         swap(1, j).wait_recv()
@@ -264,16 +275,19 @@
 
     for g in (1, 2, 3):
         img_z(g).wait_recv()
-        for d in (2, 1, 3):
+        for d in (1, 3):
             go(img_y(g, d))
+    forward_y(0)
     forward_core(0)
     forward_x(2)
     forward_x(3)
+    for g in (1, 2, 3):
+        forward_y(g)
     forward_x(1)
     forward_core(2)
     for g in range(4):
-        for d in (1, 2, 3):
-            img_y(g, d).wait_recv()
+        for h in range(2):
+            img_far(g, h).wait_recv()
     got_core(2)
     pairs(2)
     give_core(2)
@@ -343,8 +357,8 @@
             vmem((2, 3, SHARD, width), BF),
             vmem((2, 4, SHARD, quarter), BF),
             pltpu.SemaphoreType.DMA((4,)),
-            pltpu.SemaphoreType.DMA((53,)),
-            pltpu.SemaphoreType.DMA((53,)),
+            pltpu.SemaphoreType.DMA((57,)),
+            pltpu.SemaphoreType.DMA((57,)),
             pltpu.SemaphoreType.DMA((40,)),
             pltpu.SemaphoreType.DMA((40,)),
         ],

time: 104 us -> 104 us (level)
  no operation moved by 1% of the time
where the time goes in v5:
time: 104 us; the launch traced here: 103 us
  Pallas kernels  99.3 us (95%)
  between operations  1.93 us (2%)
  other arithmetic  1.8 us (2%)
    pallas_call x1, Pallas kernels, body(): pl.pallas_call(kernel, out_shape=[jax.ShapeDtypeStruct((padded, quarter),...  99.3 us

profile of v5, /device:TPU:1, one launch (start us, length us, event | category | flops | bytes accessed | tf_op | source)
XLA Modules:
  0.0 103.0 jit_solution(13073182769167110522)
XLA Ops:
  1.9 99.3 %shard_map.59 = (bf16[192,288]{1,0:T(8,128)(2,1)}, bf16[192,288]{1,0:T(8,128)(2,1)}) custom-call(f32[1]{0:T(128)S(6)} %copy.6.scale_in, f32[1]{0:T(128)S(6)} %copy.7.bias_in, bf16[176,288]{1,0:T(8,128)(2,1)} %img_in.1, bf16[176,288]{1,0:T(8,128)(2,1)} %txt_in.1), custom_call_target="tpu_custom_call" | custom-call | tf_op jit(solution)/shard_map/pallas_call | solution.py:334
  101.2 1.8 %slice_convert_fusion = (f32[176,288]{1,0:T(8,128)}, f32[176,288]{1,0:T(8,128)}) fusion(bf16[192,288]{1,0:T(8,128)(2,1)} %get-tuple-element.5, bf16[192,288]{1,0:T(8,128)(2,1)} %get-tuple-element.4), kind=kLoop, calls=%fused_computation | loop fusion | flops 101376 | bytes 608256 | tf_op jit(solution)/shard_map/convert_element_type | solution.py:369
